TPU v7x, 32 devices: a whole 2x2x4 slice. The times are simulated.
32 devices in a mesh: grp: 4 (over y, core), dev: 8 (over z, x).
Axes of the slice: x: 2, y: 2, z: 4, core: 2. Of those that a mesh axis runs over, the one named last changes fastest.
Arguments:
- video: float32 [64, 48, 1024], P(('grp', 'dev')), may hold values from -6 to 6
- measured: float32 [64, 48, 1024], P(('grp', 'dev')), may hold values from -6 to 6
- multiplier_tv: float32 [3, 64, 48, 1024], P(None, ('grp', 'dev')), may hold values from -3 to 3
- multiplier_fit: float32 [64, 48, 1024], P(('grp', 'dev')), may hold values from -6 to 6
- counts: int32 [64, 48], P(('grp', 'dev')), may hold values from 64 to 448
- ranking: int32 [1024], replicated, may hold values from 0 to 1023, each once
Outputs:
- video_next: float32 [64, 48, 1024], P(('grp', 'dev'))
- tv_next: float32 [3, 64, 48, 1024], P(None, ('grp', 'dev'))
- fit_next: float32 [64, 48, 1024], P(('grp', 'dev'))
All inputs are finite; a program needn't handle non-finite values.
Results may differ from a plain program's by a relative error of at most 0.00005.
Values sent between devices are 32-bit elements; how exact they have to be, the bound alone decides.
A program may use at most 64 MiB of HBM per device.

v0:
```python
import math

import jax
import jax.numpy as jnp
from jax import lax
from jax.sharding import PartitionSpec as P

penalty_tv = 0.5
penalty_fit = 1.0
step_size = 0.2


def swapped(value, axis, stride):
    mask = 2**stride
    pairs = [(source, source ^ mask) for source in range(lax.axis_size(axis))]
    return lax.ppermute(value, axis, pairs)


def passed_along(value, axis, steps):
    count = lax.axis_size(axis)
    pairs = [(source, (source + steps) % count) for source in range(count)]
    return lax.ppermute(value, axis, pairs)


def sign_table(size_n):
    left = lax.broadcasted_iota(jnp.int32, (size_n, size_n), 0)
    right = lax.broadcasted_iota(jnp.int32, (size_n, size_n), 1)
    common = jnp.bitwise_and(left, right)
    total = jnp.zeros((size_n, size_n), jnp.int32)
    for bit_index in range(max(size_n.bit_length(), 1)):
        total = total + jnp.bitwise_and(jnp.right_shift(common, bit_index), 1)
    return (1 - 2 * jnp.bitwise_and(total, 1)).astype(jnp.float32)


def pair_steps(field, axis_kind):
    count = lax.axis_size("dev") if axis_kind == "dev" else lax.axis_size("grp")
    for bit_index in range(count.bit_length() - 1):
        if axis_kind == "dev":
            partner = swapped(field, "dev", bit_index)
            my_bit = jnp.bitwise_and(jnp.right_shift(lax.axis_index("dev"), bit_index), 1)
        else:
            partner = swapped(field, "grp", bit_index)
            my_bit = jnp.bitwise_and(jnp.right_shift(lax.axis_index("grp"), bit_index), 1)
        field = jnp.where(my_bit == 1, partner - field, field + partner)
    return field


def time_local(field, table_t):
    return jnp.einsum("st,trc->src", table_t, field, precision=lax.Precision.HIGHEST)


def transform(field):
    frames, rows, columns = field.shape
    dev_count = lax.axis_size("dev")
    grp_count = lax.axis_size("grp")
    total_frames = frames * dev_count * grp_count
    scale = 1.0 / math.sqrt(total_frames * columns)
    table_w = sign_table(columns)
    mixed = jnp.dot(field.reshape(-1, columns), table_w, precision=lax.Precision.HIGHEST).reshape(
        field.shape
    )
    mixed = time_local(mixed, sign_table(frames))
    mixed = pair_steps(mixed, "dev")
    mixed = pair_steps(mixed, "grp")
    return mixed * scale


def gradient(field):
    after = passed_along(field[:1], ("grp", "dev"), -1)
    extended = jnp.concatenate([field[1:], after], axis=0)
    return jnp.stack(
        [extended - field, jnp.roll(field, -1, 1) - field, jnp.roll(field, -1, 2) - field]
    )


def adjoint_tv(tension):
    before = passed_along(tension[0, -1:], ("grp", "dev"), 1)
    previous = jnp.concatenate([before, tension[0, :-1]], axis=0)
    return (
        previous
        - tension[0]
        + jnp.roll(tension[1], 1, 1)
        - tension[1]
        + jnp.roll(tension[2], 1, 2)
        - tension[2]
    )


def body(video, measured, multiplier_tv, multiplier_fit, counts, ranking):
    mask = (ranking[None, None, :] < counts[:, :, None]).astype(jnp.float32)
    slopes = gradient(video)
    shifted = slopes - multiplier_tv / penalty_tv
    length = jnp.sqrt(jnp.sum(shifted * shifted, axis=0))
    shrunk = shifted * (
        jnp.maximum(length - 1.0 / penalty_tv, 0.0) / jnp.maximum(length, 1.0 / penalty_tv)
    )
    tension = penalty_tv * (slopes - shrunk) - multiplier_tv
    weighted = mask * (penalty_fit * (transform(video) - measured) - multiplier_fit)
    descent = adjoint_tv(tension) + transform(weighted)
    video_next = video - step_size * descent
    tv_next = multiplier_tv - penalty_tv * (gradient(video_next) - shrunk)
    fit_next = multiplier_fit - penalty_fit * mask * (transform(video_next) - measured)
    return (video_next, tv_next, fit_next)


def solution(mesh):
    placed = (
        P(("grp", "dev"), None, None),
        P(("grp", "dev"), None, None),
        P(None, ("grp", "dev"), None, None),
        P(("grp", "dev"), None, None),
        P(("grp", "dev"), None),
        P(),
    )
    return jax.shard_map(
        body,
        mesh=mesh,
        in_specs=placed,
        out_specs=(
            P(("grp", "dev"), None, None),
            P(None, ("grp", "dev"), None, None),
            P(("grp", "dev"), None, None),
        ),
        check_vma=False,
    )
```

profile of v0, /device:TPU:0, one launch (start us, length us, event | category | flops | bytes accessed | tf_op | source)
XLA Modules:
  0.0 193.1 jit_solution(11589014593895572887)
XLA Ops:
  0.6 9.3 %fusion.6 = f32[1024,96]{0,1:T(8,128)S(1)} fusion(f32[96,1024]{1,0:T(8,128)} %bitcast.62), kind=kOutput, calls=%fused_computation.6 | convolution fusion | flops 1246756864 | bytes 786432 | tf_op jit(solution)/shard_map/dot_general | solution.py:59
  9.9 1.6 fusion.35
  11.6 3.0 %collective-permute-start.2 = (f32[2,48,1024]{2,1,0:T(8,128)S(1)}, f32[2,48,1024]{2,1,0:T(8,128)S(1)}, u32[]{:S(2)}, u32[]{:S(2)}) collective-permute-start(f32[2,48,1024]{2,1,0:T(8,128)S(1)} %copy.34), channel_id=1, source_target_pairs={{0,1},{1,0},{2,3},{3,2},{4,5},{5,4},{6,7},{7,6},{8,9},{9,8},{10,11... | collective-permute-start | bytes 1179656 | tf_op jit(solution)/shard_map/ppermute | solution.py:16
  14.6 9.1 %collective-permute-done.2 = f32[2,48,1024]{2,1,0:T(8,128)S(1)} collective-permute-done((f32[2,48,1024]{2,1,0:T(8,128)S(1)}, f32[2,48,1024]{2,1,0:T(8,128)S(1)}, u32[]{:S(2)}, u32[]{:S(2)}) %collective-permute-start.2) | collective-permute-done | bytes 393248 | tf_op jit(solution)/shard_map/ppermute | solution.py:16
  23.9 1.9 collective-permute-start.3
  25.8 8.5 %collective-permute-done.3 = f32[2,48,1024]{2,1,0:T(8,128)S(1)} collective-permute-done((f32[2,48,1024]{2,1,0:T(8,128)S(1)}, f32[2,48,1024]{2,1,0:T(8,128)S(1)}, u32[]{:S(2)}, u32[]{:S(2)}) %collective-permute-start.3) | collective-permute-done | bytes 393248 | tf_op jit(solution)/shard_map/ppermute | solution.py:16
  34.3 2.6 %collective-permute-start.4 = (f32[2,48,1024]{2,1,0:T(8,128)S(1)}, f32[2,48,1024]{2,1,0:T(8,128)S(1)}, u32[]{:S(2)}, u32[]{:S(2)}) collective-permute-start(f32[2,48,1024]{2,1,0:T(8,128)S(1)} %add_select_fusion.10), channel_id=1, source_target_pairs={{0,4},{1,5},{2,6},{3,7},{4,0},{5,1},{6,2},{7,3},{8,12},{9,13},{10,... | collective-permute-start | bytes 1179656 | tf_op jit(solution)/shard_map/ppermute | solution.py:16
  36.9 16.2 %collective-permute-done.4 = f32[2,48,1024]{2,1,0:T(8,128)S(1)} collective-permute-done((f32[2,48,1024]{2,1,0:T(8,128)S(1)}, f32[2,48,1024]{2,1,0:T(8,128)S(1)}, u32[]{:S(2)}, u32[]{:S(2)}) %collective-permute-start.4) | collective-permute-done | bytes 393248 | tf_op jit(solution)/shard_map/ppermute | solution.py:16
  53.2 1.7 collective-permute-done.5
  55.0 1.2 collective-permute-start.6
  56.2 10.0 %collective-permute-done.6 = f32[2,48,1024]{2,1,0:T(8,128)S(1)} collective-permute-done((f32[2,48,1024]{2,1,0:T(8,128)S(1)}, f32[2,48,1024]{2,1,0:T(8,128)S(1)}, u32[]{:S(2)}, u32[]{:S(2)}) %collective-permute-start.6) | collective-permute-done | bytes 393248 | tf_op jit(solution)/shard_map/ppermute | solution.py:16
  66.2 7.7 %fusion.2 = f32[2,48,1024]{2,1,0:T(8,128)S(1)} fusion(f32[2,48,1024]{2,1,0:T(8,128)S(1)} %copy-done.4, f32[2,48,1024]{2,1,0:T(8,128)S(1)} %copy-done.5, f32[2,48,1024]{2,1,0:T(8,128)S(1)} %add_select_fusion.8, f32[2,48,1024]{2,1,0:T(8,128)S(1)} %collective-permute-done.6, s32[2,48]{1,0:T(2,128)S(1)} %copy-done.7, s32[1024]{0:T(1024)S(1)} %copy-done.6, ...), kind=kOutput, calls=%fused_computation.2 | convolution fusion | flops 1247543296 | bytes 1970561 | tf_op jit(solution)/shard_map/dot_general | solution.py:59
  73.9 1.6 fusion.33
  75.6 1.4 collective-permute-start.7
  77.0 9.2 %collective-permute-done.7 = f32[2,48,1024]{2,1,0:T(8,128)S(1)} collective-permute-done((f32[2,48,1024]{2,1,0:T(8,128)S(1)}, f32[2,48,1024]{2,1,0:T(8,128)S(1)}, u32[]{:S(2)}, u32[]{:S(2)}) %collective-permute-start.7) | collective-permute-done | bytes 393248 | tf_op jit(solution)/shard_map/ppermute | solution.py:16
  86.8 2.8 %collective-permute-start = (f32[1,48,1024]{2,1,0:T(8,128)S(1)}, f32[1,48,1024]{2,1,0:T(8,128)S(1)}, u32[]{:S(2)}, u32[]{:S(2)}) collective-permute-start(f32[1,48,1024]{2,1,0:T(8,128)S(1)} %get-tuple-element.19), channel_id=1, source_target_pairs={{0,31},{1,0},{2,1},{3,2},{4,3},{5,4},{6,5},{7,6},{8,7},{9,8},{10,9... | collective-permute-start | bytes 589832 | tf_op jit(solution)/shard_map/ppermute | solution.py:22
  89.8 11.2 %collective-permute-done.8 = f32[2,48,1024]{2,1,0:T(8,128)S(1)} collective-permute-done((f32[2,48,1024]{2,1,0:T(8,128)S(1)}, f32[2,48,1024]{2,1,0:T(8,128)S(1)}, u32[]{:S(2)}, u32[]{:S(2)}) %collective-permute-start.8) | collective-permute-done | bytes 393248 | tf_op jit(solution)/shard_map/ppermute | solution.py:16
  102.7 11.4 %collective-permute-done.9 = f32[2,48,1024]{2,1,0:T(8,128)S(1)} collective-permute-done((f32[2,48,1024]{2,1,0:T(8,128)S(1)}, f32[2,48,1024]{2,1,0:T(8,128)S(1)}, u32[]{:S(2)}, u32[]{:S(2)}) %collective-permute-start.9) | collective-permute-done | bytes 393248 | tf_op jit(solution)/shard_map/ppermute | solution.py:16
  114.7 1.2 collective-permute-done.10
  115.9 1.6 collective-permute-start.11
  118.6 8.9 %collective-permute-done.1 = f32[1,48,1024]{2,1,0:T(8,128)S(1)} collective-permute-done((f32[1,48,1024]{2,1,0:T(8,128)S(1)}, f32[1,48,1024]{2,1,0:T(8,128)S(1)}, u32[]{:S(2)}, u32[]{:S(2)}) %collective-permute-start.1) | collective-permute-done | bytes 196640 | tf_op jit(solution)/shard_map/ppermute | solution.py:22
  127.6 1.7 collective-permute-done.11
  129.7 8.0 %fusion = f32[2,48,1024]{2,1,0:T(8,128)S(1)} fusion(f32[2,48,1024]{2,1,0:T(8,128)S(1)} %fusion.18), kind=kOutput, calls=%fused_computation | convolution fusion | flops 1246756864 | bytes 786432 | tf_op jit(solution)/shard_map/dot_general | solution.py:59
  137.7 1.6 fusion.31
  139.5 10.3 %collective-permute-done.13 = f32[2,48,1024]{2,1,0:T(8,128)S(1)} collective-permute-done((f32[2,48,1024]{2,1,0:T(8,128)S(1)}, f32[2,48,1024]{2,1,0:T(8,128)S(1)}, u32[]{:S(2)}, u32[]{:S(2)}) %collective-permute-start.13) | collective-permute-done | bytes 393248 | tf_op jit(solution)/shard_map/ppermute | solution.py:16
  150.0 9.4 %collective-permute-done.14 = f32[2,48,1024]{2,1,0:T(8,128)S(1)} collective-permute-done((f32[2,48,1024]{2,1,0:T(8,128)S(1)}, f32[2,48,1024]{2,1,0:T(8,128)S(1)}, u32[]{:S(2)}, u32[]{:S(2)}) %collective-permute-start.14) | collective-permute-done | bytes 393248 | tf_op jit(solution)/shard_map/ppermute | solution.py:16
  159.5 1.7 collective-permute-start.15
  161.2 16.1 %collective-permute-done.15 = f32[2,48,1024]{2,1,0:T(8,128)S(1)} collective-permute-done((f32[2,48,1024]{2,1,0:T(8,128)S(1)}, f32[2,48,1024]{2,1,0:T(8,128)S(1)}, u32[]{:S(2)}, u32[]{:S(2)}) %collective-permute-start.15) | collective-permute-done | bytes 393248 | tf_op jit(solution)/shard_map/ppermute | solution.py:16
  177.8 4.3 %collective-permute-start.12 = (f32[1,48,1024]{2,1,0:T(8,128)S(1)}, f32[1,48,1024]{2,1,0:T(8,128)S(1)}, u32[]{:S(2)}, u32[]{:S(2)}) collective-permute-start(f32[1,48,1024]{2,1,0:T(8,128)S(1)} %get-tuple-element.14), channel_id=1, source_target_pairs={{0,31},{1,0},{2,1},{3,2},{4,3},{5,4},{6,5},{7,6},{8,7},{9,8},{10,9... | collective-permute-start | bytes 589832 | tf_op jit(solution)/shard_map/ppermute | solution.py:22
  182.7 3.0 %collective-permute-done.12 = f32[1,48,1024]{2,1,0:T(8,128)S(1)} collective-permute-done((f32[1,48,1024]{2,1,0:T(8,128)S(1)}, f32[1,48,1024]{2,1,0:T(8,128)S(1)}, u32[]{:S(2)}, u32[]{:S(2)}) %collective-permute-start.12) | collective-permute-done | bytes 196640 | tf_op jit(solution)/shard_map/ppermute | solution.py:22
  185.9 1.4 fusion.9
  187.3 5.0 %collective-permute-done.17 = f32[2,48,1024]{2,1,0:T(8,128)S(1)} collective-permute-done((f32[2,48,1024]{2,1,0:T(8,128)S(1)}, f32[2,48,1024]{2,1,0:T(8,128)S(1)}, u32[]{:S(2)}, u32[]{:S(2)}) %collective-permute-start.17) | collective-permute-done | bytes 393248 | tf_op jit(solution)/shard_map/ppermute | solution.py:16
  (64 shorter events, 7.7 us)
Async XLA Ops:
  11.6 12.1 %collective-permute-start.2 = (f32[2,48,1024]{2,1,0:T(8,128)S(1)}, f32[2,48,1024]{2,1,0:T(8,128)S(1)}, u32[]{:S(2)}, u32[]{:S(2)}) collective-permute-start(f32[2,48,1024]{2,1,0:T(8,128)S(1)} %copy.34), channel_id=1, source_target_pairs={{0,1},{1,0},{2,3},{3,2},{4,5},{5,4},{6,7},{7,6},{8,9},{9,8},{10,11... | collective-permute-start | bytes 1179656 | tf_op jit(solution)/shard_map/ppermute | solution.py:16
  23.9 10.4 %collective-permute-start.3 = (f32[2,48,1024]{2,1,0:T(8,128)S(1)}, f32[2,48,1024]{2,1,0:T(8,128)S(1)}, u32[]{:S(2)}, u32[]{:S(2)}) collective-permute-start(f32[2,48,1024]{2,1,0:T(8,128)S(1)} %add_select_fusion.11), channel_id=1, source_target_pairs={{0,2},{1,3},{2,0},{3,1},{4,6},{5,7},{6,4},{7,5},{8,10},{9,11},{10,... | collective-permute-start | bytes 1179656 | tf_op jit(solution)/shard_map/ppermute | solution.py:16
  34.3 18.8 %collective-permute-start.4 = (f32[2,48,1024]{2,1,0:T(8,128)S(1)}, f32[2,48,1024]{2,1,0:T(8,128)S(1)}, u32[]{:S(2)}, u32[]{:S(2)}) collective-permute-start(f32[2,48,1024]{2,1,0:T(8,128)S(1)} %add_select_fusion.10), channel_id=1, source_target_pairs={{0,4},{1,5},{2,6},{3,7},{4,0},{5,1},{6,2},{7,3},{8,12},{9,13},{10,... | collective-permute-start | bytes 1179656 | tf_op jit(solution)/shard_map/ppermute | solution.py:16
  36.9 29.3 %copy-start.4 = (f32[2,48,1024]{2,1,0:T(8,128)S(1)}, f32[2,48,1024]{2,1,0:T(8,128)}, u32[]{:S(2)}) copy-start(f32[2,48,1024]{2,1,0:T(8,128)} %param.9) | copy-start | bytes 1179652
  36.9 29.3 %copy-start.5 = (f32[2,48,1024]{2,1,0:T(8,128)S(1)}, f32[2,48,1024]{2,1,0:T(8,128)}, u32[]{:S(2)}) copy-start(f32[2,48,1024]{2,1,0:T(8,128)} %param.7) | copy-start | bytes 1179652
  36.9 29.3 %copy-start.6 = (s32[1024]{0:T(1024)S(1)}, s32[1024]{0:T(1024)}, u32[]{:S(2)}) copy-start(s32[1024]{0:T(1024)} %param.11) | copy-start | bytes 12292
  36.9 29.3 %copy-start.7 = (s32[2,48]{1,0:T(2,128)S(1)}, s32[2,48]{1,0:T(2,128)}, u32[]{:S(2)}) copy-start(s32[2,48]{1,0:T(2,128)} %param.10) | copy-start | bytes 1156
  53.1 1.8 collective-permute-start.5
  55.0 11.2 %collective-permute-start.6 = (f32[2,48,1024]{2,1,0:T(8,128)S(1)}, f32[2,48,1024]{2,1,0:T(8,128)S(1)}, u32[]{:S(2)}, u32[]{:S(2)}) collective-permute-start(f32[2,48,1024]{2,1,0:T(8,128)S(1)} %add_select_fusion.8), channel_id=1, source_target_pairs={{0,16},{8,24},{16,0},{24,8},{1,17},{9,25},{17,1},{25,9},{2,18},{10... | collective-permute-start | bytes 1179656 | tf_op jit(solution)/shard_map/ppermute | solution.py:16
  75.5 11.2 %copy-start.1 = (f32[2,48,1024]{2,1,0:T(8,128)S(1)}, f32[2,48,1024]{2,1,0:T(8,128)}, u32[]{:S(2)}) copy-start(f32[2,48,1024]{2,1,0:T(8,128)} %param.6) | copy-start | bytes 1179652
  75.6 10.6 %collective-permute-start.7 = (f32[2,48,1024]{2,1,0:T(8,128)S(1)}, f32[2,48,1024]{2,1,0:T(8,128)S(1)}, u32[]{:S(2)}, u32[]{:S(2)}) collective-permute-start(f32[2,48,1024]{2,1,0:T(8,128)S(1)} %copy.37), channel_id=1, source_target_pairs={{0,1},{1,0},{2,3},{3,2},{4,5},{5,4},{6,7},{7,6},{8,9},{9,8},{10,11... | collective-permute-start | bytes 1179656 | tf_op jit(solution)/shard_map/ppermute | solution.py:16
  86.4 14.6 %collective-permute-start.8 = (f32[2,48,1024]{2,1,0:T(8,128)S(1)}, f32[2,48,1024]{2,1,0:T(8,128)S(1)}, u32[]{:S(2)}, u32[]{:S(2)}) collective-permute-start(f32[2,48,1024]{2,1,0:T(8,128)S(1)} %add_select_fusion.7), channel_id=1, source_target_pairs={{0,2},{1,3},{2,0},{3,1},{4,6},{5,7},{6,4},{7,5},{8,10},{9,11},{10,... | collective-permute-start | bytes 1179656 | tf_op jit(solution)/shard_map/ppermute | solution.py:16
  86.8 14.4 %collective-permute-start = (f32[1,48,1024]{2,1,0:T(8,128)S(1)}, f32[1,48,1024]{2,1,0:T(8,128)S(1)}, u32[]{:S(2)}, u32[]{:S(2)}) collective-permute-start(f32[1,48,1024]{2,1,0:T(8,128)S(1)} %get-tuple-element.19), channel_id=1, source_target_pairs={{0,31},{1,0},{2,1},{3,2},{4,3},{5,4},{6,5},{7,6},{8,7},{9,8},{10,9... | collective-permute-start | bytes 589832 | tf_op jit(solution)/shard_map/ppermute | solution.py:22
  101.1 13.0 %collective-permute-start.9 = (f32[2,48,1024]{2,1,0:T(8,128)S(1)}, f32[2,48,1024]{2,1,0:T(8,128)S(1)}, u32[]{:S(2)}, u32[]{:S(2)}) collective-permute-start(f32[2,48,1024]{2,1,0:T(8,128)S(1)} %add_select_fusion.6), channel_id=1, source_target_pairs={{0,4},{1,5},{2,6},{3,7},{4,0},{5,1},{6,2},{7,3},{8,12},{9,13},{10,... | collective-permute-start | bytes 1179656 | tf_op jit(solution)/shard_map/ppermute | solution.py:16
  101.1 1.3 copy-start
  114.1 1.8 collective-permute-start.10
  115.9 13.3 %collective-permute-start.11 = (f32[2,48,1024]{2,1,0:T(8,128)S(1)}, f32[2,48,1024]{2,1,0:T(8,128)S(1)}, u32[]{:S(2)}, u32[]{:S(2)}) collective-permute-start(f32[2,48,1024]{2,1,0:T(8,128)S(1)} %add_select_fusion.4), channel_id=1, source_target_pairs={{0,16},{8,24},{16,0},{24,8},{1,17},{9,25},{17,1},{25,9},{2,18},{10... | collective-permute-start | bytes 1179656 | tf_op jit(solution)/shard_map/ppermute | solution.py:16
  117.6 10.0 %collective-permute-start.1 = (f32[1,48,1024]{2,1,0:T(8,128)S(1)}, f32[1,48,1024]{2,1,0:T(8,128)S(1)}, u32[]{:S(2)}, u32[]{:S(2)}) collective-permute-start(f32[1,48,1024]{2,1,0:T(8,128)S(1)} %get-tuple-element.8), channel_id=1, source_target_pairs={{0,1},{1,2},{2,3},{3,4},{4,5},{5,6},{6,7},{7,8},{8,9},{9,10},{10,1... | collective-permute-start | bytes 589832 | tf_op jit(solution)/shard_map/ppermute | solution.py:22
  129.7 48.0 %copy-start.2 = (f32[2,48,1024]{2,1,0:T(8,128)}, f32[2,48,1024]{2,1,0:T(8,128)S(1)}, u32[]{:S(2)}) copy-start(f32[2,48,1024]{2,1,0:T(8,128)S(1)} %fusion.18) | copy-start | bytes 1179652
  139.4 10.4 %collective-permute-start.13 = (f32[2,48,1024]{2,1,0:T(8,128)S(1)}, f32[2,48,1024]{2,1,0:T(8,128)S(1)}, u32[]{:S(2)}, u32[]{:S(2)}) collective-permute-start(f32[2,48,1024]{2,1,0:T(8,128)S(1)} %copy.40), channel_id=1, source_target_pairs={{0,1},{1,0},{2,3},{3,2},{4,5},{5,4},{6,7},{7,6},{8,9},{9,8},{10,11... | collective-permute-start | bytes 1179656 | tf_op jit(solution)/shard_map/ppermute | solution.py:16
  150.0 9.5 %collective-permute-start.14 = (f32[2,48,1024]{2,1,0:T(8,128)S(1)}, f32[2,48,1024]{2,1,0:T(8,128)S(1)}, u32[]{:S(2)}, u32[]{:S(2)}) collective-permute-start(f32[2,48,1024]{2,1,0:T(8,128)S(1)} %add_select_fusion.3), channel_id=1, source_target_pairs={{0,2},{1,3},{2,0},{3,1},{4,6},{5,7},{6,4},{7,5},{8,10},{9,11},{10,... | collective-permute-start | bytes 1179656 | tf_op jit(solution)/shard_map/ppermute | solution.py:16
  159.5 17.9 %collective-permute-start.15 = (f32[2,48,1024]{2,1,0:T(8,128)S(1)}, f32[2,48,1024]{2,1,0:T(8,128)S(1)}, u32[]{:S(2)}, u32[]{:S(2)}) collective-permute-start(f32[2,48,1024]{2,1,0:T(8,128)S(1)} %add_select_fusion.2), channel_id=1, source_target_pairs={{0,4},{1,5},{2,6},{3,7},{4,0},{5,1},{6,2},{7,3},{8,12},{9,13},{10,... | collective-permute-start | bytes 1179656 | tf_op jit(solution)/shard_map/ppermute | solution.py:16
  177.4 4.6 %collective-permute-start.16 = (f32[2,48,1024]{2,1,0:T(8,128)S(1)}, f32[2,48,1024]{2,1,0:T(8,128)S(1)}, u32[]{:S(2)}, u32[]{:S(2)}) collective-permute-start(f32[2,48,1024]{2,1,0:T(8,128)S(1)} %add_select_fusion.1), channel_id=1, source_target_pairs={{0,8},{8,0},{16,24},{24,16},{1,9},{9,1},{17,25},{25,17},{2,10},{10... | collective-permute-start | bytes 1179656 | tf_op jit(solution)/shard_map/ppermute | solution.py:16
  177.8 8.0 %copy-start.3 = (f32[2,48,1024]{2,1,0:T(8,128)S(1)}, f32[2,48,1024]{2,1,0:T(8,128)}, u32[]{:S(2)}) copy-start(f32[2,48,1024]{2,1,0:T(8,128)} %copy-done.2) | copy-start | bytes 1179652
  177.8 7.9 %slice-start = ((f32[2,48,1024]{2,1,0:T(8,128)}), f32[2,48,1]{2,1,0:T(8,128)S(1)}, s32[]{:S(2)}) async-start(f32[2,48,1024]{2,1,0:T(8,128)} %copy-done.2), calls=%async_computation | async-start | bytes 98304 | tf_op jit(solution)/shard_map/jit(_roll_static)/slice | solution.py:72
  177.8 7.9 %collective-permute-start.12 = (f32[1,48,1024]{2,1,0:T(8,128)S(1)}, f32[1,48,1024]{2,1,0:T(8,128)S(1)}, u32[]{:S(2)}, u32[]{:S(2)}) collective-permute-start(f32[1,48,1024]{2,1,0:T(8,128)S(1)} %get-tuple-element.14), channel_id=1, source_target_pairs={{0,31},{1,0},{2,1},{3,2},{4,3},{5,4},{6,5},{7,6},{8,7},{9,8},{10,9... | collective-permute-start | bytes 589832 | tf_op jit(solution)/shard_map/ppermute | solution.py:22
  182.1 10.2 %collective-permute-start.17 = (f32[2,48,1024]{2,1,0:T(8,128)S(1)}, f32[2,48,1024]{2,1,0:T(8,128)S(1)}, u32[]{:S(2)}, u32[]{:S(2)}) collective-permute-start(f32[2,48,1024]{2,1,0:T(8,128)S(1)} %add_select_fusion), channel_id=1, source_target_pairs={{0,16},{8,24},{16,0},{24,8},{1,17},{9,25},{17,1},{25,9},{2,18},{10... | collective-permute-start | bytes 1179656 | tf_op jit(solution)/shard_map/ppermute | solution.py:16
where the time goes:
time: 193 us
  waiting for transfers between devices  133 us (69%)
  matrix products  29.6 us (15%)
  starting transfers between devices  22.6 us (12%)
  other arithmetic  4.66 us (2%)
  local copies, waits for them, and re-layouts  2.22 us (1%)
    ppermute x15, waiting for transfers between devices, swapped(): return lax.ppermute(value, axis, pairs)  121 us
    dot_general x3, matrix products, transform(): jnp.dot(field.reshape(-1, columns), table_w, precision=lax.Precision.HIGH...  25 us
    ppermute x15, starting transfers between devices, swapped(): return lax.ppermute(value, axis, pairs)  14.7 us
    ppermute x3, waiting for transfers between devices, passed_along(): return lax.ppermute(value, axis, pairs)  12 us
    ppermute x3, starting transfers between devices, passed_along(): return lax.ppermute(value, axis, pairs)  7.9 us
    dot_general x3, matrix products, time_local(): jnp.einsum('st,trc->src', table_t, field, precision=lax.Precision.HIGHEST)  4.68 us
  transfers between devices with their start and end apart: 18, of which 16 were waited for; matrix products, arithmetic and copies ran while one was open for 2% of the time, Pallas kernels for 0%

commit v1 on v0

--- a/solution.py
+++ b/solution.py
@@ -1,8 +1,11 @@
+import functools
 import math
 
 import jax
 import jax.numpy as jnp
 from jax import lax
+from jax.experimental import pallas as pl
+from jax.experimental.pallas import tpu as pltpu
 from jax.sharding import PartitionSpec as P
 
 penalty_tv = 0.5
@@ -103,6 +106,299 @@
     return (video_next, tv_next, fit_next)
 
 
+LANES = 128
+USED = 112
+GROUPS = 4
+ROW_GROUPS = 8
+CHUNKS = GROUPS * ROW_GROUPS
+MESH_ID = pl.DeviceIdType.MESH
+
+
+def walsh(value):
+    size = value.shape[0]
+    tail = value.shape[1:]
+    half = 1
+    while half < size:
+        pairs = value.reshape((size // (2 * half), 2, half) + tail)
+        low, high = pairs[:, 0:1], pairs[:, 1:2]
+        value = jnp.concatenate([low + high, low - high], axis=1).reshape((size,) + tail)
+        half *= 2
+    return value
+
+
+def halves(value):
+    high = value.astype(jnp.bfloat16)
+    low = (value - high.astype(jnp.float32)).astype(jnp.bfloat16)
+    return jnp.concatenate([high, low], axis=0)
+
+
+def times_transposed(value, table):
+    out = lax.dot_general(
+        halves(value), table, (((1,), (1,)), ((), ())), preferred_element_type=jnp.float32
+    )
+    return out[: value.shape[0]] + out[value.shape[0] :]
+
+
+def times(value, table):
+    out = jnp.dot(halves(value), table, preferred_element_type=jnp.float32)
+    return out[: value.shape[0]] + out[value.shape[0] :]
+
+
+def kernel(
+    dev_count, count, scale,
+    video, measured, mult_tv, mult_fit, counts, ranking,
+    video_next, tv_next, fit_next,
+    select, signs, mat, mat3, part, tens,
+    s_v, s_q, s_u, s_t, s_e,
+    r_v, r_q, r_u, r_t, r_e,
+    h_v, h_t, h_u, weighted, known, keep,
+    send_sem, recv_sem, halo_send, halo_recv,
+):
+    rows, columns = video.shape[1], video.shape[2]
+    span = rows // ROW_GROUPS
+    me = lax.axis_index("grp") * dev_count + lax.axis_index("dev")
+    after = lax.rem(me + 1, count)
+    before = lax.rem(me + count - 1, count)
+
+    def coords(index):
+        return (index // dev_count, lax.rem(index, dev_count))
+
+    barrier = pltpu.get_barrier_semaphore()
+
+    def greet(step, carry):
+        other = lax.rem(me + step, count)
+        pl.semaphore_signal(barrier, inc=1, device_id=coords(other), device_id_type=MESH_ID)
+        return carry
+
+    lax.fori_loop(1, count, greet, 0)
+
+    def halo(slot, source, target, other):
+        copy = pltpu.make_async_remote_copy(
+            src_ref=source, dst_ref=target, send_sem=halo_send.at[slot],
+            recv_sem=halo_recv.at[slot], device_id=coords(other), device_id_type=MESH_ID,
+        )
+        copy.start()
+        return copy
+
+    def spread(slot, source, target):
+        def step_to(step, carry):
+            other = lax.rem(me + step, count)
+            pltpu.make_async_remote_copy(
+                src_ref=source(other), dst_ref=target.at[me], send_sem=send_sem.at[slot],
+                recv_sem=recv_sem.at[slot], device_id=coords(other), device_id_type=MESH_ID,
+            ).start()
+            return carry
+
+        lax.fori_loop(1, count, step_to, 0)
+
+    def arrived(slot, target):
+        held = target.at[pl.ds(0, count - 1)]
+        pltpu.make_async_copy(held, held, recv_sem.at[slot]).wait()
+
+    def sent(slot, target):
+        held = target.at[pl.ds(0, count - 1)]
+        pltpu.make_async_copy(held, held, send_sem.at[slot]).wait()
+
+    def cut(value, target):
+        mat[...] = value
+        for chunk in range(CHUNKS):
+            row, lane = chunk // GROUPS * span, chunk % GROUPS * LANES
+            for frame in range(2):
+                start = frame * rows + row
+                target[chunk, frame] = mat[start : start + span, lane : lane + LANES]
+
+    def paste(source, target, frames):
+        for chunk in range(CHUNKS):
+            row, lane = chunk // GROUPS * span, chunk % GROUPS * LANES
+            for frame in range(frames):
+                start = frame * rows + row
+                target[start : start + span, lane : lane + LANES] = source[chunk, frame]
+
+    wide = GROUPS * LANES
+    place = lax.broadcasted_iota(jnp.int32, (wide, LANES), 0)
+    inner = lax.rem(place, LANES)
+    rank = jnp.where(inner < USED, place // LANES * USED + inner, -1)
+    lane_index = lax.broadcasted_iota(jnp.int32, (wide, LANES), 1)
+    picked = jnp.zeros((wide, LANES), jnp.int32)
+    for tile in range(columns // LANES):
+        cols = slice(tile * LANES, (tile + 1) * LANES)
+        hit = ranking[:, cols] == rank
+        select[:, cols] = jnp.where(hit, 1.0, 0.0).astype(jnp.bfloat16)
+        picked = picked + jnp.where(hit, lane_index + tile * LANES, 0)
+    column = jnp.sum(picked.astype(jnp.float32), axis=1, keepdims=True).astype(jnp.int32)
+    common = jnp.bitwise_and(column, lane_index)
+    for shift in (4, 2, 1):
+        common = jnp.bitwise_xor(common, jnp.right_shift(common, shift))
+    low_sign = (1 - 2 * jnp.bitwise_and(common, 1)).astype(jnp.float32)
+    for tile in range(columns // LANES):
+        high = jnp.bitwise_and(jnp.right_shift(column, LANES.bit_length() - 1), tile)
+        for shift in (4, 2, 1):
+            high = jnp.bitwise_xor(high, jnp.right_shift(high, shift))
+        sign = (1 - 2 * jnp.bitwise_and(high, 1)).astype(jnp.float32)
+        signs[:, tile * LANES : (tile + 1) * LANES] = (low_sign * sign).astype(jnp.bfloat16)
+
+    pl.semaphore_wait(barrier, count - 1)
+    halo_v = halo(0, video.at[0], h_v, before)
+
+    flat = (2 * rows, columns)
+    cut(times_transposed(video[...].reshape(flat), signs[...]), s_v)
+    spread(0, lambda other: s_v.at[other], r_v)
+    r_v[me] = s_v[me]
+
+    square = (rows, rows)
+    diagonal = lax.broadcasted_iota(jnp.int32, square, 0) == lax.broadcasted_iota(
+        jnp.int32, square, 1
+    )
+    kept = []
+    for frame in range(2):
+        line = counts[frame : frame + 1, :].astype(jnp.float32)
+        kept.append(jnp.sum(jnp.where(diagonal, line, 0.0), axis=1, keepdims=True))
+    kept = jnp.concatenate(kept, axis=0)
+    wanted = times_transposed((measured[...] + mult_fit[...]).reshape(flat), select[...])
+    spare = lax.rem(lax.broadcasted_iota(jnp.int32, wanted.shape, 1), LANES) >= USED
+    cut(jnp.where(spare, kept, wanted), s_q)
+    spread(1, lambda other: s_q.at[other], r_q)
+    r_q[me] = s_q[me]
+    mask = ranking[...].astype(jnp.float32) < kept
+    known[...] = mult_fit[...].reshape(flat) + jnp.where(mask, measured[...].reshape(flat), 0.0)
+
+    halo_v.wait()
+    for frame in (1, 0):
+        here = video[frame]
+        ahead = h_v[...] if frame == 1 else video[1]
+        slopes = (
+            ahead - here,
+            pltpu.roll(here, rows - 1, 0) - here,
+            pltpu.roll(here, columns - 1, 1) - here,
+        )
+        shifted = [slopes[k] - mult_tv[k, frame] / penalty_tv for k in range(3)]
+        length = jnp.sqrt(
+            shifted[0] * shifted[0] + shifted[1] * shifted[1] + shifted[2] * shifted[2]
+        )
+        edge = 1.0 / penalty_tv
+        factor = jnp.maximum(length - edge, 0.0) / jnp.maximum(length, edge)
+        for k in range(3):
+            shrunk = shifted[k] * factor
+            tens[k, frame] = penalty_tv * (slopes[k] - shrunk) - mult_tv[k, frame]
+            part[k, frame] = mult_tv[k, frame] + penalty_tv * shrunk
+        if frame == 1:
+            halo_t = halo(1, tens.at[0, 1], h_t, after)
+
+    arrived(0, r_v)
+    arrived(1, r_q)
+    chunk_shape = (2 * count, span, LANES)
+    spectrum = walsh(r_v[...].reshape(chunk_shape)) * scale
+    wish = r_q[...].reshape(chunk_shape)
+    lanes = lax.broadcasted_iota(jnp.int32, chunk_shape, 2)
+    own_rank = (lax.rem(me, GROUPS) * USED + lanes).astype(jnp.float32)
+    inside = jnp.logical_and(lanes < USED, own_rank < wish[:, :, LANES - 1 :])
+    keep[...] = jnp.where(inside, 1.0, 0.0)
+    fresh = jnp.where(inside, spectrum - wish, 0.0) * penalty_fit
+    weighted[...] = fresh
+    back = walsh(fresh) * (scale * step_size)
+    s_t[: 2 * count] = back
+    s_t[2 * count :] = back[:1]
+    spread(2, lambda other: s_t.at[pl.ds(2 * other, 3)], r_t)
+    r_t[me] = s_t[pl.ds(2 * me, 3)]
+
+    halo_t.wait()
+    for frame in range(2):
+        previous = h_t[...] if frame == 0 else tens[0, 0]
+        adjoint = (
+            previous
+            - tens[0, frame]
+            + pltpu.roll(tens[1, frame], 1, 0)
+            - tens[1, frame]
+            + pltpu.roll(tens[2, frame], 1, 1)
+            - tens[2, frame]
+        )
+        tens[1 + frame, 0] = video[frame] - step_size * adjoint
+    halo_u = halo(2, tens.at[1, 0], h_u, before)
+    stepped = jnp.concatenate([tens[1, 0], tens[2, 0]], axis=0)
+    cut(times_transposed(stepped, signs[...]), s_u)
+    spread(3, lambda other: s_u.at[other], r_u)
+    r_u[me] = s_u[me]
+
+    arrived(3, r_u)
+    spectrum = walsh(r_u[...].reshape(chunk_shape)) * scale
+    left = keep[...] * penalty_fit * (spectrum - step_size * weighted[...])
+    s_e[...] = left.reshape(s_e.shape)
+    spread(4, lambda other: s_e.at[other], r_e)
+    r_e[me] = s_e[me]
+
+    arrived(2, r_t)
+    paste(r_t, mat3, 3)
+    change = times(mat3[...], signs[...])
+    halo_u.wait()
+    first = tens[1, 0] - change[:rows]
+    second = tens[2, 0] - change[rows : 2 * rows]
+    third = h_u[...] - change[2 * rows :]
+    video_next[0] = first
+    video_next[1] = second
+    for frame, here, ahead in ((0, first, second), (1, second, third)):
+        tv_next[0, frame] = part[0, frame] - penalty_tv * (ahead - here)
+        tv_next[1, frame] = part[1, frame] - penalty_tv * (pltpu.roll(here, rows - 1, 0) - here)
+        tv_next[2, frame] = part[2, frame] - penalty_tv * (pltpu.roll(here, columns - 1, 1) - here)
+
+    arrived(4, r_e)
+    paste(r_e, mat, 2)
+    fit_next[...] = (known[...] - times(mat[...], select[...])).reshape(fit_next.shape)
+
+    sent(0, r_v)
+    sent(1, r_q)
+    sent(2, r_t)
+    sent(3, r_u)
+    sent(4, r_e)
+
+
+def fused(dev_count, count, video, measured, mult_tv, mult_fit, counts, ranking):
+    frames, rows, columns = video.shape
+    span = rows // ROW_GROUPS
+    wide = GROUPS * LANES
+    f32 = jnp.float32
+    block = pltpu.VMEM((count, frames, span, LANES), f32)
+    scratch = [
+        pltpu.VMEM((wide, columns), jnp.bfloat16),
+        pltpu.VMEM((wide, columns), jnp.bfloat16),
+        pltpu.VMEM((frames * rows, wide), f32),
+        pltpu.VMEM(((frames + 1) * rows, wide), f32),
+        pltpu.VMEM(mult_tv.shape, f32),
+        pltpu.VMEM(mult_tv.shape, f32),
+        block, block, block,
+        pltpu.VMEM((frames * count + 1, span, LANES), f32),
+        block,
+        block, block, block,
+        pltpu.VMEM((count, frames + 1, span, LANES), f32),
+        block,
+        pltpu.VMEM((rows, columns), f32),
+        pltpu.VMEM((rows, columns), f32),
+        pltpu.VMEM((rows, columns), f32),
+        pltpu.VMEM((frames * count, span, LANES), f32),
+        pltpu.VMEM((frames * rows, columns), f32),
+        pltpu.VMEM((frames * count, span, LANES), f32),
+        pltpu.SemaphoreType.DMA((5,)),
+        pltpu.SemaphoreType.DMA((5,)),
+        pltpu.SemaphoreType.DMA((3,)),
+        pltpu.SemaphoreType.DMA((3,)),
+    ]
+    scale = 1.0 / math.sqrt(frames * count * columns)
+    vmem = pl.BlockSpec(memory_space=pltpu.VMEM)
+    return pl.pallas_call(
+        functools.partial(kernel, dev_count, count, scale),
+        out_shape=(
+            jax.ShapeDtypeStruct(video.shape, f32),
+            jax.ShapeDtypeStruct(mult_tv.shape, f32),
+            jax.ShapeDtypeStruct(video.shape, f32),
+        ),
+        in_specs=[vmem] * 6,
+        out_specs=(vmem, vmem, vmem),
+        scratch_shapes=scratch,
+        compiler_params=pltpu.CompilerParams(
+            collective_id=0, has_side_effects=True, vmem_limit_bytes=48 * 2**20
+        ),
+    )(video, measured, mult_tv, mult_fit, counts, ranking.reshape(1, columns))
+
+
 def solution(mesh):
     placed = (
         P(("grp", "dev"), None, None),
@@ -112,8 +408,11 @@
         P(("grp", "dev"), None),
         P(),
     )
+    dev_count = mesh.shape["dev"]
+    count = dev_count * mesh.shape["grp"]
+    local = functools.partial(fused, dev_count, count) if count == CHUNKS else body
     return jax.shard_map(
-        body,
+        local,
         mesh=mesh,
         in_specs=placed,
         out_specs=(

time: 193 us -> 55 us (0.28)
  waiting for transfers between devices: 133 us -> 0 us
  Pallas kernels: 0 us -> 45.9 us
  matrix products: 29.6 us -> 0 us
  starting transfers between devices: 22.6 us -> 0 us
  local copies, waits for them, and re-layouts: 2.22 us -> 8.12 us
  other arithmetic: 4.66 us -> 0 us
    ppermute x18 -> x0, waiting for transfers between devices: 133 us -> none  [the longest x15 121 us: swapped(): return lax.ppermute(value, axis, pairs)]
    pallas_call x0 -> x1, Pallas kernels: none -> 45.9 us  [fused(): pl.pallas_call(functools.partial(kernel, dev_count, count, scale), out_sh...]
    dot_general x6 -> x0, matrix products: 29.6 us -> none  [the longest x3 25 us: transform(): jnp.dot(field.reshape(-1, columns), table_w, precision=lax.Precision.HIGH...]
    ppermute x18 -> x0, starting transfers between devices: 22.6 us -> none  [the longest x15 14.7 us: swapped(): return lax.ppermute(value, axis, pairs)]
    unnamed x16 -> x15, local copies, waits for them, and re-layouts: 1.15 us -> 8.12 us
    sub x4 -> x0, other arithmetic: 3.03 us -> none  [the longest x1 1.45 us: body(): tv_next = multiplier_tv - penalty_tv * (gradient(video_next) - shrunk)]
  transfers between devices with their start and end apart: 18 -> 0, of which waited for: 16 -> 0; matrix products, arithmetic and copies ran while one was open for 2% -> 0% of each run, Pallas kernels for 0% -> 0%
where the time goes in v1:
time: 55 us; the launch traced here: 54.7 us
  Pallas kernels  45.9 us (83%)
  local copies, waits for them, and re-layouts  8.12 us (15%)
  between operations  0.65 us (1%)
    pallas_call x1, Pallas kernels, fused(): pl.pallas_call(functools.partial(kernel, dev_count, count, scale), out_sh...  45.9 us
    unnamed x15, local copies, waits for them, and re-layouts  8.12 us

profile of v1, /device:TPU:0, one launch (start us, length us, event | category | flops | bytes accessed | tf_op | source)
XLA Modules:
  0.0 54.7 jit_solution(3884816522503856763)
XLA Ops:
  0.6 0.0 copy-start
  0.6 1.3 %copy-done = f32[3,2,48,1024]{3,2,1,0:T(8,128)S(1)} copy-done((f32[3,2,48,1024]{3,2,1,0:T(8,128)S(1)}, f32[3,2,48,1024]{3,2,1,0:T(8,128)}, u32[]{:S(2)}) %copy-start) | copy-done | bytes 1179672
  1.9 0.0 copy-start.1
  1.9 1.0 %copy-done.1 = f32[2,48,1024]{2,1,0:T(8,128)S(1)} copy-done((f32[2,48,1024]{2,1,0:T(8,128)S(1)}, f32[2,48,1024]{2,1,0:T(8,128)}, u32[]{:S(2)}) %copy-start.1) | copy-done | bytes 393240
  2.9 0.0 copy-start.2
  2.9 1.0 %copy-done.2 = f32[2,48,1024]{2,1,0:T(8,128)S(1)} copy-done((f32[2,48,1024]{2,1,0:T(8,128)S(1)}, f32[2,48,1024]{2,1,0:T(8,128)}, u32[]{:S(2)}) %copy-start.2) | copy-done | bytes 393240
  3.9 0.0 copy-start.3
  3.9 1.0 %copy-done.3 = f32[2,48,1024]{2,1,0:T(8,128)S(1)} copy-done((f32[2,48,1024]{2,1,0:T(8,128)S(1)}, f32[2,48,1024]{2,1,0:T(8,128)}, u32[]{:S(2)}) %copy-start.3) | copy-done | bytes 393240
  4.9 0.0 copy-start.4
  4.9 0.7 %copy-done.4 = s32[1024]{0:T(1024)S(1)} copy-done((s32[1024]{0:T(1024)S(1)}, s32[1024]{0:T(1024)}, u32[]{:S(2)}) %copy-start.4) | copy-done | bytes 4120
  5.6 0.0 copy-start.5
  5.6 0.7 %copy-done.5 = s32[2,48]{1,0:T(2,128)S(1)} copy-done((s32[2,48]{1,0:T(2,128)S(1)}, s32[2,48]{1,0:T(2,128)}, u32[]{:S(2)}) %copy-start.5) | copy-done | bytes 408
  6.3 45.9 %shard_map.85 = (f32[2,48,1024]{2,1,0:T(8,128)S(1)}, f32[3,2,48,1024]{3,2,1,0:T(8,128)S(1)}, f32[2,48,1024]{2,1,0:T(8,128)S(1)}) custom-call(f32[2,48,1024]{2,1,0:T(8,128)S(1)} %copy-done.1, f32[2,48,1024]{2,1,0:T(8,128)S(1)} %copy-done.2, f32[3,2,48,1024]{3,2,1,0:T(8,128)S(1)} %copy-done, f32[2,48,1024]{2,1,0:T(8,128)S(1)} %copy-done.3, ...), custom_call_target="tpu_custom_call" | custom-call | tf_op jit(solution)/shard_map/pallas_call | solution.py:386
  52.2 0.7 %copy.12 = f32[2,48,1024]{2,1,0:T(8,128)} copy(f32[2,48,1024]{2,1,0:T(8,128)S(1)} %get-tuple-element.6) | data formatting | bytes 786432
  52.9 1.0 %copy.13 = f32[3,2,48,1024]{3,2,1,0:T(8,128)} copy(f32[3,2,48,1024]{3,2,1,0:T(8,128)S(1)} %get-tuple-element.7) | data formatting | bytes 2359296
  54.0 0.7 %copy.14 = f32[2,48,1024]{2,1,0:T(8,128)} copy(f32[2,48,1024]{2,1,0:T(8,128)S(1)} %get-tuple-element.8) | data formatting | bytes 786432
Async XLA Ops:
  0.6 1.3 %copy-start = (f32[3,2,48,1024]{3,2,1,0:T(8,128)S(1)}, f32[3,2,48,1024]{3,2,1,0:T(8,128)}, u32[]{:S(2)}) copy-start(f32[3,2,48,1024]{3,2,1,0:T(8,128)} %mult_tv.1) | copy-start | bytes 3538948
  1.9 1.0 %copy-start.1 = (f32[2,48,1024]{2,1,0:T(8,128)S(1)}, f32[2,48,1024]{2,1,0:T(8,128)}, u32[]{:S(2)}) copy-start(f32[2,48,1024]{2,1,0:T(8,128)} %video.1) | copy-start | bytes 1179652
  2.9 1.0 %copy-start.2 = (f32[2,48,1024]{2,1,0:T(8,128)S(1)}, f32[2,48,1024]{2,1,0:T(8,128)}, u32[]{:S(2)}) copy-start(f32[2,48,1024]{2,1,0:T(8,128)} %measured.1) | copy-start | bytes 1179652
  3.9 1.0 %copy-start.3 = (f32[2,48,1024]{2,1,0:T(8,128)S(1)}, f32[2,48,1024]{2,1,0:T(8,128)}, u32[]{:S(2)}) copy-start(f32[2,48,1024]{2,1,0:T(8,128)} %mult_fit.1) | copy-start | bytes 1179652
  4.9 0.7 %copy-start.4 = (s32[1024]{0:T(1024)S(1)}, s32[1024]{0:T(1024)}, u32[]{:S(2)}) copy-start(s32[1024]{0:T(1024)} %param.11) | copy-start | bytes 12292
  5.6 0.7 %copy-start.5 = (s32[2,48]{1,0:T(2,128)S(1)}, s32[2,48]{1,0:T(2,128)}, u32[]{:S(2)}) copy-start(s32[2,48]{1,0:T(2,128)} %counts.1) | copy-start | bytes 1156

commit v2 on v1

--- a/solution.py
+++ b/solution.py
@@ -146,13 +146,14 @@
 
 def kernel(
     dev_count, count, scale,
+    video_in, measured_in, mult_tv_in, mult_fit_in, counts_in, ranking_in,
+    video_next, tv_next, fit_next,
     video, measured, mult_tv, mult_fit, counts, ranking,
-    video_next, tv_next, fit_next,
-    select, signs, mat, mat3, part, tens,
+    select, signs, mat, part, tens, moved,
     s_v, s_q, s_u, s_t, s_e,
     r_v, r_q, r_u, r_t, r_e,
     h_v, h_t, h_u, weighted, known, keep,
-    send_sem, recv_sem, halo_send, halo_recv,
+    load_sem, send_sem, recv_sem, halo_send, halo_recv,
 ):
     rows, columns = video.shape[1], video.shape[2]
     span = rows // ROW_GROUPS
@@ -162,6 +163,22 @@
 
     def coords(index):
         return (index // dev_count, lax.rem(index, dev_count))
+
+    loads = [
+        pltpu.make_async_copy(source, target, load_sem.at[slot])
+        for slot, (source, target) in enumerate(
+            (
+                (ranking_in, ranking),
+                (counts_in, counts),
+                (video_in, video),
+                (mult_tv_in, mult_tv),
+                (measured_in, measured),
+                (mult_fit_in, mult_fit),
+            )
+        )
+    ]
+    for load in loads:
+        load.start()
 
     barrier = pltpu.get_barrier_semaphore()
 
@@ -180,24 +197,32 @@
         copy.start()
         return copy
 
-    def spread(slot, source, target):
+    def spread(slot, source, target, frame=None):
         def step_to(step, carry):
             other = lax.rem(me + step, count)
             pltpu.make_async_remote_copy(
-                src_ref=source(other), dst_ref=target.at[me], send_sem=send_sem.at[slot],
+                src_ref=source(other),
+                dst_ref=target.at[me] if frame is None else target.at[me, frame],
+                send_sem=send_sem.at[slot],
                 recv_sem=recv_sem.at[slot], device_id=coords(other), device_id_type=MESH_ID,
             ).start()
             return carry
 
         lax.fori_loop(1, count, step_to, 0)
 
-    def arrived(slot, target):
-        held = target.at[pl.ds(0, count - 1)]
+    def arrived(slot, target, frame=None):
+        held = target.at[pl.ds(0, count - 1)] if frame is None else target.at[pl.ds(0, count - 1), frame]
         pltpu.make_async_copy(held, held, recv_sem.at[slot]).wait()
 
-    def sent(slot, target):
-        held = target.at[pl.ds(0, count - 1)]
+    def sent(slot, target, frame=None):
+        held = target.at[pl.ds(0, count - 1)] if frame is None else target.at[pl.ds(0, count - 1), frame]
         pltpu.make_async_copy(held, held, send_sem.at[slot]).wait()
+
+    def cut_frame(value, target, frame):
+        mat[:rows] = value
+        for chunk in range(CHUNKS):
+            row, lane = chunk // GROUPS * span, chunk % GROUPS * LANES
+            target[chunk, frame] = mat[row : row + span, lane : lane + LANES]
 
     def cut(value, target):
         mat[...] = value
@@ -214,6 +239,15 @@
                 start = frame * rows + row
                 target[start : start + span, lane : lane + LANES] = source[chunk, frame]
 
+    pl.semaphore_wait(barrier, count - 1)
+    piece = rows // 2
+    pieces = [pl.ds(0, piece), pl.ds(piece, piece)]
+    halo_v = [
+        halo(n, video_in.at[0, cut_rows], h_v.at[cut_rows], before)
+        for n, cut_rows in enumerate(pieces)
+    ]
+
+    loads[0].wait()
     wide = GROUPS * LANES
     place = lax.broadcasted_iota(jnp.int32, (wide, LANES), 0)
     inner = lax.rem(place, LANES)
@@ -237,14 +271,14 @@
         sign = (1 - 2 * jnp.bitwise_and(high, 1)).astype(jnp.float32)
         signs[:, tile * LANES : (tile + 1) * LANES] = (low_sign * sign).astype(jnp.bfloat16)
 
-    pl.semaphore_wait(barrier, count - 1)
-    halo_v = halo(0, video.at[0], h_v, before)
-
     flat = (2 * rows, columns)
+    loads[2].wait()
     cut(times_transposed(video[...].reshape(flat), signs[...]), s_v)
     spread(0, lambda other: s_v.at[other], r_v)
     r_v[me] = s_v[me]
 
+    for load in (loads[1], loads[4], loads[5]):
+        load.wait()
     square = (rows, rows)
     diagonal = lax.broadcasted_iota(jnp.int32, square, 0) == lax.broadcasted_iota(
         jnp.int32, square, 1
@@ -257,21 +291,14 @@
     wanted = times_transposed((measured[...] + mult_fit[...]).reshape(flat), select[...])
     spare = lax.rem(lax.broadcasted_iota(jnp.int32, wanted.shape, 1), LANES) >= USED
     cut(jnp.where(spare, kept, wanted), s_q)
-    spread(1, lambda other: s_q.at[other], r_q)
-    r_q[me] = s_q[me]
-    mask = ranking[...].astype(jnp.float32) < kept
-    known[...] = mult_fit[...].reshape(flat) + jnp.where(mask, measured[...].reshape(flat), 0.0)
-
-    halo_v.wait()
-    for frame in (1, 0):
-        here = video[frame]
-        ahead = h_v[...] if frame == 1 else video[1]
-        slopes = (
-            ahead - here,
-            pltpu.roll(here, rows - 1, 0) - here,
-            pltpu.roll(here, columns - 1, 1) - here,
-        )
-        shifted = [slopes[k] - mult_tv[k, frame] / penalty_tv for k in range(3)]
+
+    loads[3].wait()
+
+    def shrink(frame, where, ahead, down, right):
+        here = video[frame, where]
+        slopes = (ahead - here, down - here, right - here)
+        mult = [mult_tv[k, frame, where] for k in range(3)]
+        shifted = [slopes[k] - mult[k] / penalty_tv for k in range(3)]
         length = jnp.sqrt(
             shifted[0] * shifted[0] + shifted[1] * shifted[1] + shifted[2] * shifted[2]
         )
@@ -279,10 +306,45 @@
         factor = jnp.maximum(length - edge, 0.0) / jnp.maximum(length, edge)
         for k in range(3):
             shrunk = shifted[k] * factor
-            tens[k, frame] = penalty_tv * (slopes[k] - shrunk) - mult_tv[k, frame]
-            part[k, frame] = mult_tv[k, frame] + penalty_tv * shrunk
-        if frame == 1:
-            halo_t = halo(1, tens.at[0, 1], h_t, after)
+            tens[k, frame, where] = penalty_tv * (slopes[k] - shrunk) - mult[k]
+            part[k, frame, where] = mult[k] + penalty_tv * shrunk
+
+    def rolled(frame):
+        here = video[frame]
+        return pltpu.roll(here, rows - 1, 0), pltpu.roll(here, columns - 1, 1)
+
+    shrink(0, pl.ds(0, rows), video[1], *rolled(0))
+    down, right = rolled(1)
+    halo_t = []
+    for n, where in enumerate(pieces):
+        halo_v[n].wait()
+        span_rows = slice(n * piece, (n + 1) * piece)
+        shrink(1, where, h_v[where], down[span_rows], right[span_rows])
+        halo_t.append(halo(2 + n, tens.at[0, 1, where], h_t.at[where], after))
+    spread(1, lambda other: s_q.at[other], r_q)
+    r_q[me] = s_q[me]
+
+    def stepped(frame, previous):
+        adjoint = (
+            previous
+            - tens[0, frame]
+            + pltpu.roll(tens[1, frame], 1, 0)
+            - tens[1, frame]
+            + pltpu.roll(tens[2, frame], 1, 1)
+            - tens[2, frame]
+        )
+        result = video[frame] - step_size * adjoint
+        moved[frame] = result
+        cut_frame(times_transposed(result, signs[...]), s_u, frame)
+        spread(3 + frame, lambda other: s_u.at[other, frame], r_u, frame)
+        r_u[me, frame] = s_u[me, frame]
+
+    stepped(1, tens[0, 0])
+    mask = ranking[...].astype(jnp.float32) < kept
+    known[...] = mult_fit[...].reshape(flat) + jnp.where(mask, measured[...].reshape(flat), 0.0)
+    halo_t[0].wait()
+    halo_t[1].wait()
+    stepped(0, h_t[...])
 
     arrived(0, r_v)
     arrived(1, r_q)
@@ -296,59 +358,43 @@
     fresh = jnp.where(inside, spectrum - wish, 0.0) * penalty_fit
     weighted[...] = fresh
     back = walsh(fresh) * (scale * step_size)
-    s_t[: 2 * count] = back
-    s_t[2 * count :] = back[:1]
-    spread(2, lambda other: s_t.at[pl.ds(2 * other, 3)], r_t)
-    r_t[me] = s_t[pl.ds(2 * me, 3)]
-
-    halo_t.wait()
-    for frame in range(2):
-        previous = h_t[...] if frame == 0 else tens[0, 0]
-        adjoint = (
-            previous
-            - tens[0, frame]
-            + pltpu.roll(tens[1, frame], 1, 0)
-            - tens[1, frame]
-            + pltpu.roll(tens[2, frame], 1, 1)
-            - tens[2, frame]
-        )
-        tens[1 + frame, 0] = video[frame] - step_size * adjoint
-    halo_u = halo(2, tens.at[1, 0], h_u, before)
-    stepped = jnp.concatenate([tens[1, 0], tens[2, 0]], axis=0)
-    cut(times_transposed(stepped, signs[...]), s_u)
-    spread(3, lambda other: s_u.at[other], r_u)
-    r_u[me] = s_u[me]
-
-    arrived(3, r_u)
+    s_t[...] = back.reshape(s_t.shape)
+    spread(2, lambda other: s_t.at[other], r_t)
+    r_t[me] = s_t[me]
+
+    arrived(3, r_u, 0)
+    arrived(4, r_u, 1)
     spectrum = walsh(r_u[...].reshape(chunk_shape)) * scale
     left = keep[...] * penalty_fit * (spectrum - step_size * weighted[...])
     s_e[...] = left.reshape(s_e.shape)
-    spread(4, lambda other: s_e.at[other], r_e)
+    spread(5, lambda other: s_e.at[other], r_e)
     r_e[me] = s_e[me]
 
     arrived(2, r_t)
-    paste(r_t, mat3, 3)
-    change = times(mat3[...], signs[...])
-    halo_u.wait()
-    first = tens[1, 0] - change[:rows]
-    second = tens[2, 0] - change[rows : 2 * rows]
-    third = h_u[...] - change[2 * rows :]
+    paste(r_t, mat, 2)
+    change = times(mat[...], signs[...])
+    first = moved[0] - change[:rows]
+    second = moved[1] - change[rows:]
+    moved[0] = first
+    halo_u = halo(4, moved.at[0], h_u, before)
     video_next[0] = first
     video_next[1] = second
-    for frame, here, ahead in ((0, first, second), (1, second, third)):
-        tv_next[0, frame] = part[0, frame] - penalty_tv * (ahead - here)
+    for frame, here in ((0, first), (1, second)):
         tv_next[1, frame] = part[1, frame] - penalty_tv * (pltpu.roll(here, rows - 1, 0) - here)
         tv_next[2, frame] = part[2, frame] - penalty_tv * (pltpu.roll(here, columns - 1, 1) - here)
-
-    arrived(4, r_e)
+    tv_next[0, 0] = part[0, 0] - penalty_tv * (second - first)
+    arrived(5, r_e)
     paste(r_e, mat, 2)
     fit_next[...] = (known[...] - times(mat[...], select[...])).reshape(fit_next.shape)
 
+    halo_u.wait()
+    tv_next[0, 1] = part[0, 1] - penalty_tv * (h_u[...] - video_next[1])
     sent(0, r_v)
     sent(1, r_q)
     sent(2, r_t)
-    sent(3, r_u)
-    sent(4, r_e)
+    sent(3, r_u, 0)
+    sent(4, r_u, 1)
+    sent(5, r_e)
 
 
 def fused(dev_count, count, video, measured, mult_tv, mult_fit, counts, ranking):
@@ -358,28 +404,31 @@
     f32 = jnp.float32
     block = pltpu.VMEM((count, frames, span, LANES), f32)
     scratch = [
+        pltpu.VMEM(video.shape, f32),
+        pltpu.VMEM(video.shape, f32),
+        pltpu.VMEM(mult_tv.shape, f32),
+        pltpu.VMEM(video.shape, f32),
+        pltpu.VMEM(counts.shape, jnp.int32),
+        pltpu.VMEM((1, columns), jnp.int32),
         pltpu.VMEM((wide, columns), jnp.bfloat16),
         pltpu.VMEM((wide, columns), jnp.bfloat16),
         pltpu.VMEM((frames * rows, wide), f32),
-        pltpu.VMEM(((frames + 1) * rows, wide), f32),
         pltpu.VMEM(mult_tv.shape, f32),
         pltpu.VMEM(mult_tv.shape, f32),
-        block, block, block,
-        pltpu.VMEM((frames * count + 1, span, LANES), f32),
-        block,
-        block, block, block,
-        pltpu.VMEM((count, frames + 1, span, LANES), f32),
-        block,
+        pltpu.VMEM(video.shape, f32),
+        block, block, block, block, block,
+        block, block, block, block, block,
         pltpu.VMEM((rows, columns), f32),
         pltpu.VMEM((rows, columns), f32),
         pltpu.VMEM((rows, columns), f32),
         pltpu.VMEM((frames * count, span, LANES), f32),
         pltpu.VMEM((frames * rows, columns), f32),
         pltpu.VMEM((frames * count, span, LANES), f32),
+        pltpu.SemaphoreType.DMA((6,)),
+        pltpu.SemaphoreType.DMA((6,)),
+        pltpu.SemaphoreType.DMA((6,)),
         pltpu.SemaphoreType.DMA((5,)),
         pltpu.SemaphoreType.DMA((5,)),
-        pltpu.SemaphoreType.DMA((3,)),
-        pltpu.SemaphoreType.DMA((3,)),
     ]
     scale = 1.0 / math.sqrt(frames * count * columns)
     vmem = pl.BlockSpec(memory_space=pltpu.VMEM)
@@ -390,11 +439,11 @@
             jax.ShapeDtypeStruct(mult_tv.shape, f32),
             jax.ShapeDtypeStruct(video.shape, f32),
         ),
-        in_specs=[vmem] * 6,
+        in_specs=[pl.BlockSpec(memory_space=pl.ANY)] * 6,
         out_specs=(vmem, vmem, vmem),
         scratch_shapes=scratch,
         compiler_params=pltpu.CompilerParams(
-            collective_id=0, has_side_effects=True, vmem_limit_bytes=48 * 2**20
+            collective_id=0, has_side_effects=True, vmem_limit_bytes=63 * 2**20
         ),
     )(video, measured, mult_tv, mult_fit, counts, ranking.reshape(1, columns))
 

time: 55 us -> 47.7 us (0.87)
  Pallas kernels: 45.9 us -> 41.9 us
  local copies, waits for them, and re-layouts: 8.12 us -> 4.98 us
    pallas_call x1, Pallas kernels: 45.9 us -> 41.9 us  [fused(): pl.pallas_call(functools.partial(kernel, dev_count, count, scale), out_sh...]
    unnamed x15 -> x5, local copies, waits for them, and re-layouts: 8.12 us -> 4.98 us
where the time goes in v2:
time: 47.7 us; the launch traced here: 47.5 us
  Pallas kernels  41.9 us (88%)
  local copies, waits for them, and re-layouts  4.98 us (10%)
  between operations  0.64 us (1%)
    pallas_call x1, Pallas kernels, fused(): pl.pallas_call(functools.partial(kernel, dev_count, count, scale), out_sh...  41.9 us
    unnamed x5, local copies, waits for them, and re-layouts  4.98 us

profile of v2, /device:TPU:0, one launch (start us, length us, event | category | flops | bytes accessed | tf_op | source)
XLA Modules:
  0.0 47.5 jit_solution(5692324107409605442)
XLA Ops:
  0.6 41.9 %shard_map.85 = (f32[2,48,1024]{2,1,0:T(8,128)}, f32[3,2,48,1024]{3,2,1,0:T(8,128)}, f32[2,48,1024]{2,1,0:T(8,128)}) custom-call(f32[2,48,1024]{2,1,0:T(8,128)} %video_in.1, f32[2,48,1024]{2,1,0:T(8,128)} %measured_in.1, f32[3,2,48,1024]{3,2,1,0:T(8,128)} %mult_tv_in.1, f32[2,48,1024]{2,1,0:T(8,128)} %mult_fit_in.1, s32[2,48]{1,0:T(2,128)} %counts_in.1, ...), custom_call_target="tpu_custom_call" | custom-call | tf_op jit(solution)/shard_map/pallas_call | solution.py:435
  42.5 1.8 %copy.12 = f32[2,48,1024]{2,1,0:T(8,128)} copy(f32[2,48,1024]{2,1,0:T(8,128)} %get-tuple-element.6) | data formatting | bytes 786432
  44.3 0.0 copy-start
  44.3 2.5 %copy.13 = f32[3,2,48,1024]{3,2,1,0:T(8,128)} copy(f32[3,2,48,1024]{3,2,1,0:T(8,128)} %get-tuple-element.7) | data formatting | bytes 2359296
  46.7 0.0 copy-done
  46.7 0.7 %copy.14 = f32[2,48,1024]{2,1,0:T(8,128)} copy(f32[2,48,1024]{2,1,0:T(8,128)S(1)} %copy-done) | data formatting | bytes 786432
Async XLA Ops:
  44.3 2.5 %copy-start = (f32[2,48,1024]{2,1,0:T(8,128)S(1)}, f32[2,48,1024]{2,1,0:T(8,128)}, u32[]{:S(2)}) copy-start(f32[2,48,1024]{2,1,0:T(8,128)} %get-tuple-element.8) | copy-start | bytes 1179652

commit v3 on v2

--- a/solution.py
+++ b/solution.py
@@ -395,6 +395,24 @@
     sent(3, r_u, 0)
     sent(4, r_u, 1)
     sent(5, r_e)
+
+
+def place(*refs):
+    sources, targets, stages = refs[:3], refs[3:6], refs[6:9]
+    in_sem, out_sem = refs[9:]
+    loads, stores = [], []
+    for source, target, stage in zip(sources, targets, stages):
+        for n in range(source.shape[0]):
+            slot = len(loads)
+            loads.append(pltpu.make_async_copy(source.at[n], stage.at[n], in_sem.at[slot]))
+            stores.append(pltpu.make_async_copy(stage.at[n], target.at[n], out_sem.at[slot]))
+    for load in loads:
+        load.start()
+    for load, store in zip(loads, stores):
+        load.wait()
+        store.start()
+    for store in stores:
+        store.wait()
 
 
 def fused(dev_count, count, video, measured, mult_tv, mult_fit, counts, ranking):
@@ -432,13 +450,14 @@
     ]
     scale = 1.0 / math.sqrt(frames * count * columns)
     vmem = pl.BlockSpec(memory_space=pltpu.VMEM)
-    return pl.pallas_call(
+    shapes = (
+        jax.ShapeDtypeStruct(video.shape, f32),
+        jax.ShapeDtypeStruct(mult_tv.shape, f32),
+        jax.ShapeDtypeStruct(video.shape, f32),
+    )
+    results = pl.pallas_call(
         functools.partial(kernel, dev_count, count, scale),
-        out_shape=(
-            jax.ShapeDtypeStruct(video.shape, f32),
-            jax.ShapeDtypeStruct(mult_tv.shape, f32),
-            jax.ShapeDtypeStruct(video.shape, f32),
-        ),
+        out_shape=shapes,
         in_specs=[pl.BlockSpec(memory_space=pl.ANY)] * 6,
         out_specs=(vmem, vmem, vmem),
         scratch_shapes=scratch,
@@ -446,6 +465,16 @@
             collective_id=0, has_side_effects=True, vmem_limit_bytes=63 * 2**20
         ),
     )(video, measured, mult_tv, mult_fit, counts, ranking.reshape(1, columns))
+    anywhere = pl.BlockSpec(memory_space=pl.ANY)
+    return pl.pallas_call(
+        place,
+        out_shape=shapes,
+        in_specs=[anywhere] * 3,
+        out_specs=(anywhere,) * 3,
+        scratch_shapes=[pltpu.VMEM(shape.shape, f32) for shape in shapes]
+        + [pltpu.SemaphoreType.DMA((7,)), pltpu.SemaphoreType.DMA((7,))],
+        compiler_params=pltpu.CompilerParams(vmem_limit_bytes=60 * 2**20),
+    )(*results)
 
 
 def solution(mesh):

time: 47.7 us -> 45.1 us (0.945)
  local copies, waits for them, and re-layouts: 4.98 us -> 0 us
  Pallas kernels: 41.9 us -> 44.3 us
    unnamed x5 -> x0, local copies, waits for them, and re-layouts: 4.98 us -> none
    pallas_call x0 -> x1, Pallas kernels: none -> 2.45 us  [fused(): pl.pallas_call(place, out_shape=shapes, in_specs=[anywhere] * 3, out_spec...]
where the time goes in v3:
time: 45.1 us; the launch traced here: 44.9 us
  Pallas kernels  44.3 us (98%)
  between operations  0.64 us (1%)
    pallas_call x1, Pallas kernels, fused(): pl.pallas_call(functools.partial(kernel, dev_count, count, scale), out_sh...  41.9 us
    pallas_call x1, Pallas kernels, fused(): pl.pallas_call(place, out_shape=shapes, in_specs=[anywhere] * 3, out_spec...  2.45 us

profile of v3, /device:TPU:0, one launch (start us, length us, event | category | flops | bytes accessed | tf_op | source)
XLA Modules:
  0.0 44.9 jit_solution(16869048407083549533)
XLA Ops:
  0.6 41.9 %shard_map.85 = (f32[2,48,1024]{2,1,0:T(8,128)}, f32[3,2,48,1024]{3,2,1,0:T(8,128)}, f32[2,48,1024]{2,1,0:T(8,128)}) custom-call(f32[2,48,1024]{2,1,0:T(8,128)} %video_in.1, f32[2,48,1024]{2,1,0:T(8,128)} %measured_in.1, f32[3,2,48,1024]{3,2,1,0:T(8,128)} %mult_tv_in.1, f32[2,48,1024]{2,1,0:T(8,128)} %mult_fit_in.1, s32[2,48]{1,0:T(2,128)} %counts_in.1, ...), custom_call_target="tpu_custom_call" | custom-call | tf_op jit(solution)/shard_map/pallas_call | solution.py:458
  42.5 2.4 %shard_map.86 = (f32[2,48,1024]{2,1,0:T(8,128)}, f32[3,2,48,1024]{3,2,1,0:T(8,128)}, f32[2,48,1024]{2,1,0:T(8,128)}) custom-call(f32[2,48,1024]{2,1,0:T(8,128)} %get-tuple-element.6.refs_0_, f32[3,2,48,1024]{3,2,1,0:T(8,128)} %get-tuple-element.7.refs_1_, f32[2,48,1024]{2,1,0:T(8,128)} %get-tuple-element.8.refs_2_), custom_call_target="tpu_custom_call" | custom-call | tf_op jit(solution)/shard_map/pallas_call | solution.py:469

commit v4 on v3

--- a/solution.py
+++ b/solution.py
@@ -372,11 +372,10 @@
 
     arrived(2, r_t)
     paste(r_t, mat, 2)
-    change = times(mat[...], signs[...])
-    first = moved[0] - change[:rows]
-    second = moved[1] - change[rows:]
+    first = moved[0] - times(mat[:rows], signs[...])
     moved[0] = first
     halo_u = halo(4, moved.at[0], h_u, before)
+    second = moved[1] - times(mat[rows:], signs[...])
     video_next[0] = first
     video_next[1] = second
     for frame, here in ((0, first), (1, second)):

time: 45.1 us -> 45 us (level)
  no operation moved by 1% of the time
where the time goes in v4:
time: 45 us; the launch traced here: 44.9 us
  Pallas kernels  44.2 us (98%)
  between operations  0.64 us (1%)
    pallas_call x1, Pallas kernels, fused(): pl.pallas_call(functools.partial(kernel, dev_count, count, scale), out_sh...  41.8 us
    pallas_call x1, Pallas kernels, fused(): pl.pallas_call(place, out_shape=shapes, in_specs=[anywhere] * 3, out_spec...  2.45 us

profile of v4, /device:TPU:0, one launch (start us, length us, event | category | flops | bytes accessed | tf_op | source)
XLA Modules:
  0.0 44.9 jit_solution(7608352420814336834)
XLA Ops:
  0.6 41.8 %shard_map.85 = (f32[2,48,1024]{2,1,0:T(8,128)}, f32[3,2,48,1024]{3,2,1,0:T(8,128)}, f32[2,48,1024]{2,1,0:T(8,128)}) custom-call(f32[2,48,1024]{2,1,0:T(8,128)} %video_in.1, f32[2,48,1024]{2,1,0:T(8,128)} %measured_in.1, f32[3,2,48,1024]{3,2,1,0:T(8,128)} %mult_tv_in.1, f32[2,48,1024]{2,1,0:T(8,128)} %mult_fit_in.1, s32[2,48]{1,0:T(2,128)} %counts_in.1, ...), custom_call_target="tpu_custom_call" | custom-call | tf_op jit(solution)/shard_map/pallas_call | solution.py:457
  42.4 2.4 %shard_map.86 = (f32[2,48,1024]{2,1,0:T(8,128)}, f32[3,2,48,1024]{3,2,1,0:T(8,128)}, f32[2,48,1024]{2,1,0:T(8,128)}) custom-call(f32[2,48,1024]{2,1,0:T(8,128)} %get-tuple-element.6.refs_0_, f32[3,2,48,1024]{3,2,1,0:T(8,128)} %get-tuple-element.7.refs_1_, f32[2,48,1024]{2,1,0:T(8,128)} %get-tuple-element.8.refs_2_), custom_call_target="tpu_custom_call" | custom-call | tf_op jit(solution)/shard_map/pallas_call | solution.py:468
